TPU v7x, 32 devices: a whole 2x2x4 slice. The times are simulated.
32 devices in a mesh: mass: 4 (over y, x), shard: 8 (over z, core).
Axes of the slice: x: 2, y: 2, z: 4, core: 2. Of those that a mesh axis runs over, the one named last changes fastest.
Arguments:
- queries: bfloat16 [512, 8192], P(('mass', 'shard')), may hold values from -6 to 6
- library: bfloat16 [32768, 8192], P(('mass', 'shard')), may hold values from -0.0625 to 0.0625
- routes: int32 [512, 1], P(('mass', 'shard')), may hold values from 0 to 3; in each aligned block of 16 rows (0 to 15, 16 to 31, ...) at most 8 rows name the same one
- offsets: int32 [512], P(('mass', 'shard')), may hold values from -2048 to 2048
Outputs:
- best_scores: float32 [512, 16], P(('mass', 'shard'))
Inputs may be any that keep to these rules, and one draw needn't show every extreme that they name: `routes`: in each device's aligned block of 16 queries at most 8 go to one mass group, and some group gets exactly 8 from some device.
All inputs are finite; a program needn't handle non-finite values.
Results may differ from a plain program's by a relative error of at most 0.00087.
Values may be sent and summed in bfloat16 or wider, within the bound.
A program may use at most 128 MiB of HBM per device.

v0:
```python
import jax
import jax.numpy as jnp
from jax import lax
from jax.sharding import PartitionSpec as P

MAX_SHIFT = 2048
TOP_K = 16


def shifted_spectra(queries, offsets):
    row_count = queries.shape[0]
    bin_count = queries.shape[1]
    margin = jnp.zeros((row_count, MAX_SHIFT), queries.dtype)
    current = jnp.concatenate([margin, queries, margin], axis=1)
    window_start = MAX_SHIFT - offsets
    bit_total = (2 * MAX_SHIFT).bit_length()
    for bit_number in range(bit_total):
        step_size = 1 << bit_number
        moved = jnp.concatenate(
            [current[:, step_size:], jnp.zeros((row_count, step_size), current.dtype)], axis=1
        )
        taken = window_start >> bit_number & 1 == 1
        current = jnp.where(taken[:, None], moved, current)
    shifted = current[:, :bin_count]
    combined = queries.astype(jnp.float32) + shifted.astype(jnp.float32)
    scale_factor = lax.rsqrt(jnp.mean(combined * combined, axis=1, keepdims=True) + 1e-06)
    return (combined * scale_factor).astype(jnp.bfloat16)


def block_ranks(dest_group):
    length = dest_group.shape[0]
    position_ids = jnp.arange(length, dtype=jnp.int32)
    earlier = (dest_group[:, None] == dest_group[None, :]) & (
        position_ids[:, None] > position_ids[None, :]
    )
    return jnp.sum(earlier.astype(jnp.int32), axis=1)


def keep_best(values):
    return lax.top_k(values, TOP_K)[0]


def per_device(queries, library, routes, offsets):
    mass_count = lax.axis_size("mass")
    query_count = queries.shape[0]
    capacity = query_count // 2
    spectra = shifted_spectra(queries, offsets)
    dest_group = routes[:, 0]
    slot_index = dest_group * capacity + block_ranks(dest_group)
    selector = (
        jnp.arange(mass_count * capacity, dtype=jnp.int32)[:, None] == slot_index[None, :]
    ).astype(jnp.bfloat16)
    packed = jnp.dot(selector, spectra, preferred_element_type=jnp.float32).astype(jnp.bfloat16)
    arrived = lax.all_to_all(packed, "mass", split_axis=0, concat_axis=0, tiled=True)
    scores = lax.dot_general(
        lax.all_gather(arrived, "shard", axis=0, tiled=True),
        library,
        (((1,), (1,)), ((), ())),
        preferred_element_type=jnp.float32,
    )
    local_best = keep_best(scores)
    spread_lists = lax.all_to_all(local_best, "shard", split_axis=0, concat_axis=1, tiled=True)
    own_best = keep_best(spread_lists)
    returned_best = lax.all_to_all(own_best, "mass", split_axis=0, concat_axis=0, tiled=True)
    slot_match = slot_index[:, None] == jnp.arange(mass_count * capacity, dtype=jnp.int32)[None, :]
    return jnp.sum(
        jnp.where(slot_match[:, :, None], returned_best[None, :, :], jnp.float32(0.0)), axis=1
    )


def solution(mesh):
    placed = (
        P(("mass", "shard"), None),
        P(("mass", "shard"), None),
        P(("mass", "shard"), None),
        P(("mass", "shard")),
    )
    return jax.shard_map(
        per_device,
        mesh=mesh,
        in_specs=placed,
        out_specs=P(("mass", "shard"), None),
        check_vma=False,
    )
```

profile of v0, /device:TPU:0, one launch (start us, length us, event | category | flops | bytes accessed | tf_op | source)
XLA Modules:
  0.0 152.9 jit_solution(15997991219037819926)
XLA Ops:
  6.5 0.7 and_compare_fusion.12
  7.3 1.0 pad_maximum_fusion
  8.3 0.2 slice.58
  8.4 1.1 pad_select_fusion.11
  9.5 0.2 slice.59
  9.7 0.2 pad_select_fusion.10
  9.9 0.2 slice.60
  10.1 0.2 pad_select_fusion.9
  10.2 0.2 slice.61
  10.4 0.2 pad_select_fusion.8
  10.6 0.2 slice.62
  10.7 0.2 pad_select_fusion.7
  10.9 0.2 slice.63
  11.1 0.2 pad_select_fusion.6
  11.3 0.2 slice.64
  11.4 0.2 pad_select_fusion.5
  11.6 0.2 pad_select_fusion.4
  11.8 0.2 pad_select_fusion.3
  12.0 0.2 pad_select_fusion.2
  12.2 0.2 pad_select_fusion.1
  12.4 0.2 pad_select_fusion
  12.6 0.4 multiply_reduce_fusion
  13.0 0.2 convert_reduce_fusion
  13.2 0.4 fusion
  13.6 13.6 %all_to_all.40 = bf16[4,8,8192]{2,1,0:T(8,128)(2,1)} all-to-all(bf16[4,8,8192]{2,1,0:T(8,128)(2,1)S(1)} %fusion), channel_id=1, replica_groups=mesh['mass'=4,'shard'=8] {'mass'}, dimensions={0} | all-to-all | bytes 1048576 | tf_op jit(solution)/shard_map/all_to_all | solution.py:54
  27.2 0.0 all-gather.2.cloned.1.call-update
  27.2 47.0 %all-gather.2.cloned.1.call-done = bf16[256,8192]{1,0:T(8,128)(2,1)} async-done(((bf16[32,8192]{1,0:T(8,128)(2,1)}), bf16[256,8192]{1,0:T(8,128)(2,1)}) %all-gather.2.cloned.1.call-update) | async-done | bytes 4194320 | tf_op jit(solution)/shard_map/all_gather | solution.py:56
  74.2 9.3 %fusion.5 = f32[256,1024]{0,1:T(8,128)S(1)} fusion(bf16[256,8192]{1,0:T(8,128)(2,1)} %all-gather.2.cloned.1.call-done, bf16[1024,8192]{1,0:T(8,128)(2,1)} %param.5), kind=kOutput, calls=%fused_computation.46 | convolution fusion | flops 4294967296 | bytes 22020096
  83.6 0.1 iota.24.clone
  83.6 38.0 %top_k.14 = (f32[256,1024]{0,1:T(8,128)S(1)}, s32[256,1024]{0,1:T(8,128)}) sort(f32[256,1024]{0,1:T(8,128)S(1)} %fusion.5, s32[256,1024]{0,1:T(8,128)S(1)} %iota.24.clone), dimensions={1}, to_apply=%region_2.3 | sort | flops 4718592 | bytes 4194304 | tf_op jit(solution)/shard_map/top_k | solution.py:40
  121.6 0.3 copy.19
  122.0 0.1 copy.14
  122.0 0.7 reshape.62
  122.8 3.3 %all-to-all-start.1 = ((f32[8,1,512]{2,1,0:T(1,128)}), f32[8,1,512]{2,1,0:T(1,128)S(1)}, u32[]{:S(2)}, u32[]{:S(2)}) async-start(f32[8,1,512]{2,1,0:T(1,128)} %reshape.62), calls=%async_computation.1 | async-start | bytes 32768 | tf_op jit(solution)/shard_map/all_to_all | solution.py:62
  126.1 5.6 %all-to-all-done.1 = f32[8,1,512]{2,1,0:T(1,128)S(1)} async-done(((f32[8,1,512]{2,1,0:T(1,128)}), f32[8,1,512]{2,1,0:T(1,128)S(1)}, u32[]{:S(2)}, u32[]{:S(2)}) %all-to-all-start.1) | async-done | bytes 16416 | tf_op jit(solution)/shard_map/all_to_all | solution.py:62
  131.7 0.5 broadcast.203
  132.2 0.6 reduce
  132.8 0.1 reshape.63
  132.9 0.1 copy.15
  132.9 2.8 %top_k.20 = (f32[32,128]{1,0:T(8,128)S(1)}, s32[32,128]{1,0:T(8,128)}) sort(f32[32,128]{1,0:T(8,128)S(1)} %copy.15, s32[32,128]{1,0:T(8,128)S(1)} %iota.25), dimensions={1}, to_apply=%region_3.4 | sort | flops 49152 | bytes 65536 | tf_op jit(solution)/shard_map/top_k | solution.py:40
  135.8 0.7 reshape.64
  136.4 3.7 %all-to-all-start.2 = ((f32[4,1,128]{2,1,0:T(1,128)}), f32[4,1,128]{2,1,0:T(1,128)S(1)}, u32[]{:S(2)}, u32[]{:S(2)}) async-start(f32[4,1,128]{2,1,0:T(1,128)} %reshape.64), calls=%async_computation.2 | async-start | bytes 4096 | tf_op jit(solution)/shard_map/all_to_all | solution.py:64
  140.1 0.1 iota_compare_fusion.2
  140.2 4.5 %all-to-all-done.2 = f32[4,1,128]{2,1,0:T(1,128)S(1)} async-done(((f32[4,1,128]{2,1,0:T(1,128)}), f32[4,1,128]{2,1,0:T(1,128)S(1)}, u32[]{:S(2)}, u32[]{:S(2)}) %all-to-all-start.2) | async-done | bytes 2080 | tf_op jit(solution)/shard_map/all_to_all | solution.py:64
  144.7 0.6 reduce.1
  145.2 0.1 reshape.65
  145.3 0.1 copy.16
  145.4 0.7 select_reduce_fusion
  (18 shorter events, 0.2 us)
Async XLA Ops:
  6.5 6.1 %copy-start = (bf16[16,8192]{1,0:T(8,128)(2,1)S(1)}, bf16[16,8192]{1,0:T(8,128)(2,1)}, u32[]{:S(2)}) copy-start(bf16[16,8192]{1,0:T(8,128)(2,1)} %param.4) | copy-start | bytes 786436
  6.5 6.5 %copy-start.1 = (s32[16,1]{0,1:T(1,128)S(1)}, s32[16,1]{0,1:T(1,128)}, u32[]{:S(2)}) copy-start(s32[16,1]{0,1:T(1,128)} %param.6) | copy-start | bytes 196
  6.5 67.7 %all-gather.2.cloned.1.call-start = ((), (), s32[]{:S(2)}) async-start(), calls=%async_computation.3 | async-start | bytes 4718592 | tf_op jit(solution)/shard_map/all_gather | solution.py:56
  122.8 8.9 %all-to-all-start.1 = ((f32[8,1,512]{2,1,0:T(1,128)}), f32[8,1,512]{2,1,0:T(1,128)S(1)}, u32[]{:S(2)}, u32[]{:S(2)}) async-start(f32[8,1,512]{2,1,0:T(1,128)} %reshape.62), calls=%async_computation.1 | async-start | bytes 32768 | tf_op jit(solution)/shard_map/all_to_all | solution.py:62
  136.4 8.2 %all-to-all-start.2 = ((f32[4,1,128]{2,1,0:T(1,128)}), f32[4,1,128]{2,1,0:T(1,128)S(1)}, u32[]{:S(2)}, u32[]{:S(2)}) async-start(f32[4,1,128]{2,1,0:T(1,128)} %reshape.64), calls=%async_computation.2 | async-start | bytes 4096 | tf_op jit(solution)/shard_map/all_to_all | solution.py:64
Sparse Core Ops, SparseCore 0:
  27.3 46.8 all-gather.1
where the time goes:
time: 153 us
  waiting for transfers between devices  57.1 us (37%)
  other arithmetic  47.9 us (31%)
  blocking collectives  13.6 us (9%)
  between operations  13.6 us (9%)
  matrix products  9.7 us (6%)
  starting transfers between devices  6.99 us (5%)
  local copies, waits for them, and re-layouts  4.03 us (3%)
    all_gather x1, waiting for transfers between devices, per_device(): lax.all_gather(arrived, 'shard', axis=0, tiled=True)  47 us
    top_k x2, other arithmetic, keep_best(): return lax.top_k(values, TOP_K)[0]  40.8 us
    all_to_all x1, blocking collectives, per_device(): lax.all_to_all(packed, 'mass', split_axis=0, concat_axis=0, tiled=True)  13.6 us
    unnamed x1, matrix products  9.34 us
    all_to_all x1, waiting for transfers between devices, per_device(): lax.all_to_all(local_best, 'shard', split_axis=0, concat_axis=1, tiled=True)  5.57 us
    all_to_all x1, waiting for transfers between devices, per_device(): lax.all_to_all(own_best, 'mass', split_axis=0, concat_axis=0, tiled=True)  4.5 us
    all_to_all x1, starting transfers between devices, per_device(): lax.all_to_all(own_best, 'mass', split_axis=0, concat_axis=0, tiled=True)  3.65 us
    all_to_all x1, starting transfers between devices, per_device(): lax.all_to_all(local_best, 'shard', split_axis=0, concat_axis=1, tiled=True)  3.33 us
  transfers between devices with their start and end apart: 3, of which 3 were waited for; matrix products, arithmetic and copies ran while one was open for 0% of the time, Pallas kernels for 0%

commit v1 on v0

v1 whole, which is shorter than its diff:
```python
import functools

import jax
import jax.numpy as jnp
from jax import lax
from jax.experimental import pallas as pl
from jax.experimental.pallas import tpu as pltpu
from jax.sharding import PartitionSpec as P

MESH = pl.DeviceIdType.MESH
MAX_SHIFT = 2048
TOP_K = 16
LANES = 128
F32 = jnp.float32
BF16 = jnp.bfloat16


def comparators(count):
    pairs = []
    p = 1
    while p < count:
        k = p
        while k >= 1:
            for j in range(k % p, count - k, 2 * k):
                for i in range(min(k, count - j - k)):
                    if (i + j) // (2 * p) == (i + j + k) // (2 * p):
                        pairs.append((i + j, i + j + k))
            k //= 2
        p *= 2
    return pairs


def exchange(values, pairs):
    values = list(values)
    for i, j in pairs:
        a, b = values[i], values[j]
        values[i], values[j] = jnp.maximum(a, b), jnp.minimum(a, b)
    return values


SORT = comparators(TOP_K)
BITONIC = [
    (i, i + d) for d in (8, 4, 2, 1) for i in range(TOP_K) if i & d == 0
]


def merge(first, second):
    kept = [jnp.maximum(first[i], second[TOP_K - 1 - i]) for i in range(TOP_K)]
    return exchange(kept, BITONIC)


def spectra_kernel(mass_count, queries_ref, offsets_ref, routes_ref, routes_row_ref, halves_ref, own_ref):
    rows, bins = queries_ref.shape
    half = bins // 2
    capacity = rows // 2
    core = lax.rem(lax.axis_index("shard"), 2)
    plain = queries_ref[...].astype(F32)
    margin = jnp.zeros((rows, MAX_SHIFT), F32)
    current = jnp.concatenate([margin, plain, margin], axis=1)
    start = MAX_SHIFT - offsets_ref[...]
    step = 2 * MAX_SHIFT
    current = jnp.where(
        (start & step) != 0,
        jnp.concatenate([current[:, step:], jnp.zeros((rows, step), F32)], axis=1),
        current,
    )
    step //= 2
    while step >= LANES:
        width = bins + step
        current = jnp.where(
            (start & step) != 0, current[:, step : step + width], current[:, :width]
        )
        step //= 2
    width = bins + LANES
    while step >= 1:
        moved = pltpu.roll(current, width - step, 1)
        current = jnp.where((start & step) != 0, moved, current)
        step //= 2
    combined = plain + current[:, :bins]
    scale = lax.rsqrt(jnp.sum(combined * combined, axis=1, keepdims=True) * (1.0 / bins) + 1e-06)
    spectra = (combined * scale).astype(BF16)
    group = routes_ref[...]
    before = lax.broadcasted_iota(jnp.int32, (rows, rows), 0) > lax.broadcasted_iota(
        jnp.int32, (rows, rows), 1
    )
    earlier = (group == routes_row_ref[...]) & before
    rank = jnp.sum(jnp.where(earlier, 1.0, 0.0), axis=1, keepdims=True).astype(jnp.int32)
    lane = lax.broadcasted_iota(jnp.int32, (rows, LANES), 1)
    slot = group * (2 * capacity) + core * capacity + rank
    hot = jnp.where(lane == slot, 1.0, 0.0).astype(BF16)
    own_ref[...] = jnp.where(lane == group * capacity + rank, 1.0, 0.0)
    for part in range(2):
        halves_ref[part, :, :half] = spectra[:, part * half : (part + 1) * half]
        halves_ref[part, :, half:] = hot


def search_kernel(
    mass_count,
    shard_count,
    halves_ref,
    own_ref,
    library_ref,
    out_ref,
    lib,
    held,
    packed,
    slots,
    scores,
    outgoing,
    lists,
    lib_sem,
    start_sem,
    line_send,
    line_recv,
    layer_send,
    layer_recv,
    local_sem,
    pair_send,
    pair_recv,
    list_send,
    list_recv,
):
    places = shard_count // 2
    rows = halves_ref.shape[1]
    half = halves_ref.shape[2] - LANES
    cap = rows // 2
    block = mass_count * rows
    total = places * block
    mass = lax.axis_index("mass")
    shard = lax.axis_index("shard")
    place = shard // 2
    core = lax.rem(shard, 2)
    sibling = (mass, shard + 1 - 2 * core)
    device_count = mass_count * shard_count
    me = mass * shard_count + shard

    lib_copy = pltpu.make_async_copy(library_ref, lib, lib_sem)
    lib_copy.start()
    barrier = pltpu.get_barrier_semaphore()

    def greet(k, carry):
        other = lax.rem(me + k, device_count)
        pl.semaphore_signal(
            barrier,
            inc=1,
            device_id=(other // shard_count, lax.rem(other, shard_count)),
            device_id_type=MESH,
        )
        return carry

    lax.fori_loop(1, device_count, greet, 0)
    pl.semaphore_wait(barrier, device_count - 1)

    mine = pl.ds(pl.multiple_of(core * rows, rows), rows)
    swap = pltpu.make_async_remote_copy(
        src_ref=halves_ref.at[1 - core],
        dst_ref=held.at[place, mine],
        send_sem=start_sem.at[0],
        recv_sem=start_sem.at[1],
        device_id=sibling,
        device_id_type=MESH,
    )
    swap.start()
    keep = pltpu.make_async_copy(halves_ref.at[core], held.at[place, mine], start_sem.at[2])
    keep.start()
    keep.wait()
    swap.wait_recv()

    def line_copy(origin, way):
        return pltpu.make_async_remote_copy(
            src_ref=held.at[origin],
            dst_ref=held.at[origin],
            send_sem=line_send.at[way, origin],
            recv_sem=line_recv.at[origin],
            device_id=(mass, shard + (2 if way == 0 else -2)),
            device_id_type=MESH,
        )

    def layer_copy(origin, hop):
        target = lax.rem(mass + hop, mass_count)
        return pltpu.make_async_remote_copy(
            src_ref=packed.at[origin, pl.ds(pl.multiple_of(target * rows, rows), rows)],
            dst_ref=slots.at[
                core, pl.ds(pl.multiple_of(origin * block + mass * rows, rows), rows)
            ],
            send_sem=layer_send.at[origin, hop],
            recv_sem=layer_recv.at[origin, hop],
            device_id=(target, shard),
            device_id_type=MESH,
        )

    def layer_arrival(origin, hop):
        source = lax.rem(mass + mass_count - hop, mass_count)
        return pltpu.make_async_remote_copy(
            src_ref=packed.at[origin, pl.ds(0, rows)],
            dst_ref=slots.at[
                core, pl.ds(pl.multiple_of(origin * block + source * rows, rows), rows)
            ],
            send_sem=layer_send.at[origin, hop],
            recv_sem=layer_recv.at[origin, hop],
            device_id=(source, shard),
            device_id_type=MESH,
        )

    def local_copy(origin):
        return pltpu.make_async_copy(
            packed.at[origin, pl.ds(pl.multiple_of(mass * rows, rows), rows)],
            slots.at[core, pl.ds(pl.multiple_of(origin * block + mass * rows, rows), rows)],
            local_sem.at[origin],
        )

    def pair_copy(origin, part):
        span = slots.at[part, pl.ds(pl.multiple_of(origin * block, block), block)]
        return pltpu.make_async_remote_copy(
            src_ref=span,
            dst_ref=span,
            send_sem=pair_send.at[origin],
            recv_sem=pair_recv.at[origin],
            device_id=sibling,
            device_id_type=MESH,
        )

    def dispatch(origin):
        hot = held[origin, :, half:].astype(F32).T[:block].astype(BF16)
        tile = 512

        def pack(j, carry):
            span = pl.ds(pl.multiple_of(j * tile, tile), tile)
            packed[origin, :, span] = jnp.dot(
                hot, held[origin, :, span], preferred_element_type=F32
            ).astype(BF16)
            return carry

        lax.fori_loop(0, half // tile, pack, 0)
        for hop in range(1, mass_count):
            layer_copy(origin, hop).start()
        local_copy(origin).start()

    def hand_over(origin):
        local_copy(origin).wait()
        for hop in range(1, mass_count):
            layer_arrival(origin, hop).wait_recv()
        pair_copy(origin, core).start()

    @pl.when(place + 1 < places)
    def _():
        line_copy(place, 0).start()

    @pl.when(place > 0)
    def _():
        line_copy(place, 1).start()

    dispatch(place)

    def advance(t, carry):
        below, above = place - 1 - t, place + 1 + t

        @pl.when(below >= 0)
        def _():
            line_copy(below, 0).wait_recv()

            @pl.when(place + 1 < places)
            def _():
                line_copy(below, 0).start()

            dispatch(below)

        @pl.when(above < places)
        def _():
            line_copy(above, 1).wait_recv()

            @pl.when(place > 0)
            def _():
                line_copy(above, 1).start()

            dispatch(above)

        @pl.when(below + 1 >= 0)
        def _():
            hand_over(below + 1)

        @pl.when((above - 1 < places) & (t > 0))
        def _():
            hand_over(above - 1)

        return carry

    lax.fori_loop(0, places - 1, advance, 0)
    for last in (place - (places - 1), place + (places - 1)):

        @pl.when((last >= 0) & (last < places))
        def _():
            hand_over(last)

    lax.fori_loop(
        0, places, lambda o, x: (pair_copy(o, 1 - core).wait_recv(), x)[1], 0
    )
    lib_copy.wait()

    lib_rows = lib.shape[0]
    tall, wide = min(512, lib_rows), min(256, total)

    def score(k, carry):
        i, j = k // (total // wide), lax.rem(k, total // wide)
        down = pl.ds(pl.multiple_of(i * tall, tall), tall)
        across = pl.ds(pl.multiple_of(j * wide, wide), wide)
        sums = None
        for part in range(2):
            term = lax.dot_general(
                lib[down, part * half : (part + 1) * half],
                slots[part, across, :],
                (((1,), (1,)), ((), ())),
                preferred_element_type=F32,
            )
            sums = term if sums is None else sums + term
        scores[down, across] = sums
        return carry

    lax.fori_loop(0, (lib_rows // tall) * (total // wide), score, 0)

    sub = lax.broadcasted_iota(jnp.int32, (8, LANES), 0)

    def as_columns(values):
        upper, lower = values[0], values[8]
        for i in range(1, 8):
            upper = jnp.where(sub == i, values[i], upper)
            lower = jnp.where(sub == i, values[8 + i], lower)
        rest = jnp.zeros((LANES - TOP_K, LANES), F32)
        return jnp.concatenate([upper, lower, rest], axis=0).T

    stride = lib_rows // TOP_K

    def best(tile, carry):
        across = pl.ds(pl.multiple_of(tile * LANES, LANES), LANES)

        def more(r, kept):
            fresh = [
                scores[pl.ds(pl.multiple_of(i * stride + r * 8, 8), 8), across]
                for i in range(TOP_K)
            ]
            return tuple(merge(kept, exchange(fresh, SORT)))

        kept = tuple(jnp.full((8, LANES), -jnp.inf, F32) for _ in range(TOP_K))
        kept = lax.fori_loop(0, stride // 8, more, kept)
        for d in (4, 2, 1):
            kept = merge(kept, [pltpu.roll(x, d, 0) for x in kept])
        outgoing[across, :] = as_columns(kept)
        return carry

    lax.fori_loop(0, total // LANES, best, 0)

    def list_copy(k):
        other = lax.rem(me + k, device_count)
        to_mass, to_shard = other // shard_count, lax.rem(other, shard_count)
        at = ((to_shard // 2) * mass_count + to_mass) * 2 + lax.rem(to_shard, 2)
        return pltpu.make_async_remote_copy(
            src_ref=outgoing.at[pl.ds(pl.multiple_of(at * cap, cap), cap)],
            dst_ref=lists.at[
                pl.ds(pl.multiple_of((shard * mass_count + mass) * cap, cap), cap)
            ],
            send_sem=list_send.at[k],
            recv_sem=list_recv.at[k],
            device_id=(to_mass, to_shard),
            device_id_type=MESH,
        )

    def list_arrival(k):
        other = lax.rem(me + device_count - k, device_count)
        from_mass, from_shard = other // shard_count, lax.rem(other, shard_count)
        return pltpu.make_async_remote_copy(
            src_ref=outgoing.at[pl.ds(0, cap)],
            dst_ref=lists.at[
                pl.ds(pl.multiple_of((from_shard * mass_count + from_mass) * cap, cap), cap)
            ],
            send_sem=list_send.at[k],
            recv_sem=list_recv.at[k],
            device_id=(from_mass, from_shard),
            device_id_type=MESH,
        )

    lax.fori_loop(1, device_count, lambda k, x: (list_copy(k).start(), x)[1], 0)
    own_at = ((place * mass_count + mass) * 2 + core) * cap
    lists[pl.ds(pl.multiple_of((shard * mass_count + mass) * cap, cap), cap), :] = outgoing[
        pl.ds(pl.multiple_of(own_at, cap), cap), :
    ]
    lax.fori_loop(1, device_count, lambda k, x: (list_arrival(k).wait_recv(), x)[1], 0)

    kept = None
    for tile in range(device_count * cap // LANES):
        turned = lists[tile * LANES : (tile + 1) * LANES, :].T
        fresh = [jnp.broadcast_to(turned[i : i + 1, :], (8, LANES)) for i in range(TOP_K)]
        kept = fresh if kept is None else merge(kept, fresh)
    turn = mass_count * cap
    while turn < LANES:
        kept = merge(kept, [pltpu.roll(x, turn, 1) for x in kept])
        turn *= 2
    chosen = jnp.dot(
        own_ref[...],
        as_columns(kept),
        preferred_element_type=F32,
        precision=lax.Precision.HIGHEST,
    )
    out_ref[...] = chosen[:, :TOP_K]

    swap.wait_send()

    def finish(origin, carry):
        @pl.when((place + 1 < places) & (origin <= place))
        def _():
            line_copy(origin, 0).wait_send()

        @pl.when((place > 0) & (origin >= place))
        def _():
            line_copy(origin, 1).wait_send()

        for hop in range(1, mass_count):
            layer_copy(origin, hop).wait_send()
        pair_copy(origin, core).wait_send()
        return carry

    lax.fori_loop(0, places, finish, 0)
    lax.fori_loop(1, device_count, lambda k, x: (list_copy(k).wait_send(), x)[1], 0)


def per_device(mass_count, shard_count, queries, library, routes, offsets):
    rows, bins = queries.shape
    half = bins // 2
    places = shard_count // 2
    cap = rows // 2
    block = mass_count * rows
    total = places * block
    device_count = mass_count * shard_count
    vmem = pl.BlockSpec(memory_space=pltpu.VMEM)
    halves, own = pl.pallas_call(
        functools.partial(spectra_kernel, mass_count),
        out_shape=(
            jax.ShapeDtypeStruct((2, rows, half + LANES), BF16),
            jax.ShapeDtypeStruct((rows, LANES), F32),
        ),
        in_specs=[vmem] * 4,
        out_specs=(vmem, vmem),
        compiler_params=pltpu.CompilerParams(vmem_limit_bytes=32 * 2**20),
    )(queries, offsets[:, None], routes, routes.reshape(1, rows))
    dma = pltpu.SemaphoreType.DMA
    return pl.pallas_call(
        functools.partial(search_kernel, mass_count, shard_count),
        out_shape=jax.ShapeDtypeStruct((rows, TOP_K), F32),
        in_specs=[vmem, vmem, pl.BlockSpec(memory_space=pl.ANY)],
        out_specs=vmem,
        scratch_shapes=[
            pltpu.VMEM(library.shape, BF16),
            pltpu.VMEM((places, 2 * rows, half + LANES), BF16),
            pltpu.VMEM((places, block, half), BF16),
            pltpu.VMEM((2, total, half), BF16),
            pltpu.VMEM((library.shape[0], total), F32),
            pltpu.VMEM((total, LANES), F32),
            pltpu.VMEM((device_count * cap, LANES), F32),
            dma,
            dma((3,)),
            dma((2, places)),
            dma((places,)),
            dma((places, mass_count)),
            dma((places, mass_count)),
            dma((places,)),
            dma((places,)),
            dma((places,)),
            dma((device_count,)),
            dma((device_count,)),
        ],
        compiler_params=pltpu.CompilerParams(
            collective_id=0, has_side_effects=True, vmem_limit_bytes=56 * 2**20
        ),
    )(halves, own, library)


def solution(mesh):
    placed = (
        P(("mass", "shard"), None),
        P(("mass", "shard"), None),
        P(("mass", "shard"), None),
        P(("mass", "shard")),
    )
    return jax.shard_map(
        functools.partial(per_device, mesh.shape["mass"], mesh.shape["shard"]),
        mesh=mesh,
        in_specs=placed,
        out_specs=P(("mass", "shard"), None),
        check_vma=False,
    )
```

time: 153 us -> 60 us (0.39)
  waiting for transfers between devices: 57.1 us -> 0 us
  Pallas kernels: 0 us -> 54.1 us
  other arithmetic: 47.9 us -> 0 us
  blocking collectives: 13.6 us -> 0 us
  between operations: 13.6 us -> 0.03 us
  matrix products: 9.7 us -> 0 us
  starting transfers between devices: 6.99 us -> 0 us
  local copies, waits for them, and re-layouts: 4.03 us -> 5.66 us
    pallas_call x0 -> x2, Pallas kernels: none -> 54.1 us  [the longest x1 52.8 us: per_device(): pl.pallas_call(functools.partial(search_kernel, mass_count, shard_count),...]
    all_gather x1 -> x0, waiting for transfers between devices: 47 us -> none  [per_device(): lax.all_gather(arrived, 'shard', axis=0, tiled=True)]
    top_k x2 -> x0, other arithmetic: 40.8 us -> none  [keep_best(): return lax.top_k(values, TOP_K)[0]]
    all_to_all x1 -> x0, blocking collectives: 13.6 us -> none  [per_device(): lax.all_to_all(packed, 'mass', split_axis=0, concat_axis=0, tiled=True)]
    all_to_all x2 -> x0, waiting for transfers between devices: 10.1 us -> none  [the longest x1 5.57 us: per_device(): lax.all_to_all(local_best, 'shard', split_axis=0, concat_axis=1, tiled=True)]
    unnamed x1 -> x0, matrix products: 9.34 us -> none
    all_to_all x2 -> x0, starting transfers between devices: 6.99 us -> none  [the longest x1 3.65 us: per_device(): lax.all_to_all(own_best, 'mass', split_axis=0, concat_axis=0, tiled=True)]
    unnamed x8 -> x10, local copies, waits for them, and re-layouts: 1.53 us -> 4.93 us
  transfers between devices with their start and end apart: 3 -> 0, of which waited for: 3 -> 0; matrix products, arithmetic and copies ran while one was open for 0% -> 0% of each run, Pallas kernels for 0% -> 0%
where the time goes in v1:
time: 60 us; the launch traced here: 59.8 us
  Pallas kernels  54.1 us (90%)
  local copies, waits for them, and re-layouts  5.66 us (9%)
    pallas_call x1, Pallas kernels, per_device(): pl.pallas_call(functools.partial(search_kernel, mass_count, shard_count),...  52.8 us
    unnamed x10, local copies, waits for them, and re-layouts  4.93 us
    pallas_call x1, Pallas kernels, per_device(): pl.pallas_call(functools.partial(spectra_kernel, mass_count), out_shape=(...  1.29 us

profile of v1, /device:TPU:0, one launch (start us, length us, event | category | flops | bytes accessed | tf_op | source)
XLA Modules:
  0.0 59.8 jit_solution(9381260950446914556)
XLA Ops:
  0.0 0.7 %copy.5.offsets_ref = s32[16,1]{1,0:T(8,128)S(1)} copy(s32[16,1]{0,1:T(1,128)} %bitcast.3) | data formatting | bytes 128 | tf_op jit(solution)/shard_map/broadcast_in_dim | solution.py:443
  0.7 0.7 %copy.6.routes_ref = s32[16,1]{1,0:T(8,128)S(1)} copy(s32[16,1]{0,1:T(1,128)} %param.6) | data formatting | bytes 128 | tf_op args[2]
  1.5 0.0 copy-start.1
  1.5 0.9 %copy-done.1 = bf16[16,8192]{1,0:T(8,128)(2,1)S(1)} copy-done((bf16[16,8192]{1,0:T(8,128)(2,1)S(1)}, bf16[16,8192]{1,0:T(8,128)(2,1)}, u32[]{:S(2)}) %copy-start.1) | copy-done | bytes 262168
  2.4 0.0 copy-start.3
  2.4 0.7 %copy-done.3 = s32[16,1]{0,1:T(1,128)S(1)} copy-done((s32[16,1]{0,1:T(1,128)S(1)}, s32[16,1]{0,1:T(1,128)}, u32[]{:S(2)}) %copy-start.3) | copy-done | bytes 88
  3.1 1.3 %shard_map.46 = (bf16[2,16,4224]{2,1,0:T(8,128)(2,1)S(1)}, f32[16,128]{1,0:T(8,128)S(1)}) custom-call(bf16[16,8192]{1,0:T(8,128)(2,1)S(1)} %copy-done.1, s32[16,1]{1,0:T(8,128)S(1)} %copy.5.offsets_ref, s32[16,1]{1,0:T(8,128)S(1)} %copy.6.routes_ref, s32[1,16]{1,0:T(1,128)S(1)} %bitcast.2), custom_call_target="tpu_custom_call" | custom-call | tf_op jit(solution)/shard_map/pallas_call | solution.py:434
  4.4 0.0 copy-start
  4.4 0.7 %copy-done = bf16[2,16,4224]{2,1,0:T(8,128)(2,1)} copy-done((bf16[2,16,4224]{2,1,0:T(8,128)(2,1)}, bf16[2,16,4224]{2,1,0:T(8,128)(2,1)S(1)}, u32[]{:S(2)}) %copy-start) | copy-done | bytes 270360
  5.1 0.0 copy-start.2
  5.1 0.6 copy-done.2
  5.7 52.8 %shard_map.47 = f32[16,16]{1,0:T(8,128)} custom-call(bf16[2,16,4224]{2,1,0:T(8,128)(2,1)} %copy-done, f32[16,128]{1,0:T(8,128)} %copy-done.2, bf16[1024,8192]{1,0:T(8,128)(2,1)} %library_ref.1), custom_call_target="tpu_custom_call" | custom-call | tf_op jit(solution)/shard_map/pallas_call | solution.py:445
  58.5 1.3 %copy.8 = f32[16,16]{1,0:T(8,128)} copy(f32[16,16]{1,0:T(8,128)} %shard_map.47) | data formatting | bytes 2048
Async XLA Ops:
  1.5 0.9 %copy-start.1 = (bf16[16,8192]{1,0:T(8,128)(2,1)S(1)}, bf16[16,8192]{1,0:T(8,128)(2,1)}, u32[]{:S(2)}) copy-start(bf16[16,8192]{1,0:T(8,128)(2,1)} %queries_ref.1) | copy-start | bytes 786436
  2.4 0.7 %copy-start.3 = (s32[16,1]{0,1:T(1,128)S(1)}, s32[16,1]{0,1:T(1,128)}, u32[]{:S(2)}) copy-start(s32[16,1]{0,1:T(1,128)} %param.6) | copy-start | bytes 196
  4.4 0.7 %copy-start = (bf16[2,16,4224]{2,1,0:T(8,128)(2,1)}, bf16[2,16,4224]{2,1,0:T(8,128)(2,1)S(1)}, u32[]{:S(2)}) copy-start(bf16[2,16,4224]{2,1,0:T(8,128)(2,1)S(1)} %get-tuple-element.7.halves_ref) | copy-start | bytes 811012
  5.1 0.6 copy-start.2

commit v2 on v1

v2 whole, which is shorter than its diff:
```python
import functools

import jax
import jax.numpy as jnp
from jax import lax
from jax.experimental import pallas as pl
from jax.experimental.pallas import tpu as pltpu
from jax.sharding import PartitionSpec as P

MESH = pl.DeviceIdType.MESH
MAX_SHIFT = 2048
TOP_K = 16
LANES = 128
PARTS = 4
F32 = jnp.float32
BF16 = jnp.bfloat16


def comparators(count):
    pairs = []
    p = 1
    while p < count:
        k = p
        while k >= 1:
            for j in range(k % p, count - k, 2 * k):
                for i in range(min(k, count - j - k)):
                    if (i + j) // (2 * p) == (i + j + k) // (2 * p):
                        pairs.append((i + j, i + j + k))
            k //= 2
        p *= 2
    return pairs


def exchange(values, pairs):
    values = list(values)
    for i, j in pairs:
        a, b = values[i], values[j]
        values[i], values[j] = jnp.maximum(a, b), jnp.minimum(a, b)
    return values


SORT = comparators(TOP_K)
BITONIC = [
    (i, i + d) for d in (8, 4, 2, 1) for i in range(TOP_K) if i & d == 0
]


def merge(first, second):
    kept = [jnp.maximum(first[i], second[TOP_K - 1 - i]) for i in range(TOP_K)]
    return exchange(kept, BITONIC)


def spectra_parts(core, queries_ref, offsets_ref, routes_ref, halves, hots, owns):
    rows, bins = queries_ref.shape
    half = bins // 2
    parts, width = halves.shape[1], halves.shape[3]
    capacity = rows // 2
    down = lax.broadcasted_iota(jnp.int32, (rows, rows), 0)
    right = lax.broadcasted_iota(jnp.int32, (rows, rows), 1)

    def as_column(row):
        spread = jnp.broadcast_to(row.astype(F32), (rows, rows))
        return jnp.sum(jnp.where(down == right, spread, 0.0), axis=1, keepdims=True).astype(
            jnp.int32
        )

    plain = queries_ref[...].astype(F32)
    margin = jnp.zeros((rows, MAX_SHIFT), F32)
    current = jnp.concatenate([margin, plain, margin], axis=1)
    start = MAX_SHIFT - as_column(offsets_ref[...])
    step = 2 * MAX_SHIFT
    current = jnp.where(
        (start & step) != 0,
        jnp.concatenate([current[:, step:], jnp.zeros((rows, step), F32)], axis=1),
        current,
    )
    step //= 2
    while step >= LANES:
        wide = bins + step
        current = jnp.where(
            (start & step) != 0, current[:, step : step + wide], current[:, :wide]
        )
        step //= 2
    wide = bins + LANES
    while step >= 1:
        moved = pltpu.roll(current, wide - step, 1)
        current = jnp.where((start & step) != 0, moved, current)
        step //= 2
    combined = plain + current[:, :bins]
    scale = lax.rsqrt(jnp.sum(combined * combined, axis=1, keepdims=True) * (1.0 / bins) + 1e-06)
    spectra = (combined * scale).astype(BF16)
    group = as_column(routes_ref[...])
    earlier = (group == routes_ref[...]) & (down > right)
    rank = jnp.sum(jnp.where(earlier, 1.0, 0.0), axis=1, keepdims=True).astype(jnp.int32)
    lane = lax.broadcasted_iota(jnp.int32, (rows, LANES), 1)
    slot = group * (2 * capacity) + core * capacity + rank
    hots[...] = jnp.where(lane == slot, 1.0, 0.0).astype(BF16)
    owns[...] = jnp.where(lane == group * capacity + rank, 1.0, 0.0)
    for side in range(2):
        for part in range(parts):
            at = side * half + part * width
            halves[side, part] = spectra[:, at : at + width]


def search_kernel(
    mass_count,
    shard_count,
    queries_ref,
    offsets_ref,
    routes_ref,
    library_ref,
    out_ref,
    plain,
    shifts,
    groups,
    halves,
    hots,
    owns,
    lib,
    held,
    held_hots,
    packed,
    slots,
    scores,
    outgoing,
    lists,
    lib_sem,
    load_sem,
    start_sem,
    hot_send,
    hot_recv,
    line_send,
    line_recv,
    layer_send,
    layer_recv,
    pair_send,
    pair_recv,
    list_send,
    list_recv,
):
    places = shard_count // 2
    parts, rows, width = halves.shape[1:]
    half = parts * width
    cap = rows // 2
    block = mass_count * rows
    total = places * block
    mass = lax.axis_index("mass")
    shard = lax.axis_index("shard")
    place = shard // 2
    core = lax.rem(shard, 2)
    sibling = (mass, shard + 1 - 2 * core)
    device_count = mass_count * shard_count
    me = mass * shard_count + shard

    loads = [
        pltpu.make_async_copy(source, target, load_sem.at[i])
        for i, (source, target) in enumerate(
            [(queries_ref, plain), (offsets_ref, shifts), (routes_ref, groups)]
        )
    ]
    for load in loads:
        load.start()
    lib_copy = pltpu.make_async_copy(library_ref, lib, lib_sem)
    barrier = pltpu.get_barrier_semaphore()

    def greet(k, carry):
        other = lax.rem(me + k, device_count)
        pl.semaphore_signal(
            barrier,
            inc=1,
            device_id=(other // shard_count, lax.rem(other, shard_count)),
            device_id_type=MESH,
        )
        return carry

    lax.fori_loop(1, device_count, greet, 0)
    for load in loads:
        load.wait()
    lib_copy.start()
    spectra_parts(core, plain, shifts, groups, halves, hots, owns)
    pl.semaphore_wait(barrier, device_count - 1)

    mine = pl.ds(pl.multiple_of(core * rows, rows), rows)
    swap = pltpu.make_async_remote_copy(
        src_ref=halves.at[1 - core],
        dst_ref=held.at[place, :, mine, :],
        send_sem=start_sem.at[0],
        recv_sem=start_sem.at[1],
        device_id=sibling,
        device_id_type=MESH,
    )
    swap.start()
    swap_hot = pltpu.make_async_remote_copy(
        src_ref=hots,
        dst_ref=held_hots.at[place, mine, :],
        send_sem=start_sem.at[3],
        recv_sem=start_sem.at[4],
        device_id=sibling,
        device_id_type=MESH,
    )
    swap_hot.start()
    keep = pltpu.make_async_copy(halves.at[core], held.at[place, :, mine, :], start_sem.at[2])
    keep.start()
    held_hots[place, mine, :] = hots[...]
    keep.wait()
    swap_hot.wait_recv()
    swap.wait_recv()

    def hot_copy(origin, way):
        return pltpu.make_async_remote_copy(
            src_ref=held_hots.at[origin],
            dst_ref=held_hots.at[origin],
            send_sem=hot_send.at[way, origin],
            recv_sem=hot_recv.at[origin],
            device_id=(mass, shard + (2 if way == 0 else -2)),
            device_id_type=MESH,
        )

    def line_copy(origin, part, way):
        return pltpu.make_async_remote_copy(
            src_ref=held.at[origin, part],
            dst_ref=held.at[origin, part],
            send_sem=line_send.at[way, origin * parts + part],
            recv_sem=line_recv.at[origin * parts + part],
            device_id=(mass, shard + (2 if way == 0 else -2)),
            device_id_type=MESH,
        )

    def layer_rows(origin, source):
        return pl.ds(pl.multiple_of(origin * block + source * rows, rows), rows)

    def layer_copy(origin, part, hop):
        target = lax.rem(mass + hop, mass_count)
        return pltpu.make_async_remote_copy(
            src_ref=packed.at[origin, part, layer_rows(0, target)],
            dst_ref=slots.at[core, part, layer_rows(origin, mass)],
            send_sem=layer_send.at[origin * parts + part, hop],
            recv_sem=layer_recv.at[origin * parts + part, hop],
            device_id=(target, shard),
            device_id_type=MESH,
        )

    def layer_arrival(origin, part, hop):
        source = lax.rem(mass + mass_count - hop, mass_count)
        return pltpu.make_async_remote_copy(
            src_ref=packed.at[origin, part, pl.ds(0, rows)],
            dst_ref=slots.at[core, part, layer_rows(origin, source)],
            send_sem=layer_send.at[origin * parts + part, hop],
            recv_sem=layer_recv.at[origin * parts + part, hop],
            device_id=(source, shard),
            device_id_type=MESH,
        )

    def pair_copy(origin, part, side):
        span = slots.at[side, part, pl.ds(pl.multiple_of(origin * block, block), block)]
        return pltpu.make_async_remote_copy(
            src_ref=span,
            dst_ref=span,
            send_sem=pair_send.at[origin * parts + part],
            recv_sem=pair_recv.at[origin * parts + part],
            device_id=sibling,
            device_id_type=MESH,
        )

    tile = min(512, width)

    def dispatch(origin, part):
        hot = held_hots[origin].astype(F32).T[:block].astype(BF16)

        def pack(j, carry):
            span = pl.ds(pl.multiple_of(j * tile, tile), tile)
            packed[origin, part, :, span] = jnp.dot(
                hot, held[origin, part, :, span], preferred_element_type=F32
            ).astype(BF16)
            return carry

        lax.fori_loop(0, width // tile, pack, 0)
        for hop in range(1, mass_count):
            layer_copy(origin, part, hop).start()
        slots[core, part, layer_rows(origin, mass), :] = packed[
            origin, part, layer_rows(0, mass), :
        ]

    def leave(part):
        for way, there in ((0, place + 1 < places), (1, place > 0)):

            @pl.when(there)
            def _():
                if part == 0:
                    hot_copy(place, way).start()
                line_copy(place, part, way).start()

    def take(origin, part, way, there):
        if part == 0:
            hot_copy(origin, way).wait_recv()
        line_copy(origin, part, way).wait_recv()

        @pl.when(there)
        def _():
            if part == 0:
                hot_copy(origin, way).start()
            line_copy(origin, part, way).start()

        dispatch(origin, part)

    def gather(part):
        if part + 2 < parts:
            leave(part + 2)
        dispatch(place, part)

        def advance(t, carry):
            below, above = place - 1 - t, place + 1 + t

            @pl.when(below >= 0)
            def _():
                take(below, part, 0, place + 1 < places)

            @pl.when(above < places)
            def _():
                take(above, part, 1, place > 0)

            return carry

        lax.fori_loop(0, places - 1, advance, 0)

    def hand_over(part):
        def one(origin):
            for hop in range(1, mass_count):
                layer_arrival(origin, part, hop).wait_recv()
            pair_copy(origin, part, core).start()

        one(place)

        def advance(t, carry):
            for origin in (place - 1 - t, place + 1 + t):

                @pl.when((origin >= 0) & (origin < places))
                def _():
                    one(origin)

            return carry

        lax.fori_loop(0, places - 1, advance, 0)

    lib_rows = lib.shape[0]
    tall, wide = min(512, lib_rows), min(256, total)

    def multiply(part):
        lax.fori_loop(
            0, places, lambda o, x: (pair_copy(o, part, 1 - core).wait_recv(), x)[1], 0
        )

        def score(k, carry):
            i, j = k // (total // wide), lax.rem(k, total // wide)
            down = pl.ds(pl.multiple_of(i * tall, tall), tall)
            across = pl.ds(pl.multiple_of(j * wide, wide), wide)
            sums = None if part == 0 else scores[down, across]
            for side in range(2):
                at = side * half + part * width
                term = lax.dot_general(
                    lib[down, at : at + width],
                    slots[side, part, across, :],
                    (((1,), (1,)), ((), ())),
                    preferred_element_type=F32,
                )
                sums = term if sums is None else sums + term
            scores[down, across] = sums
            return carry

        lax.fori_loop(0, (lib_rows // tall) * (total // wide), score, 0)

    for part in range(min(2, parts)):
        leave(part)
    for step in range(parts + 2):
        if step < parts:
            gather(step)
        if 0 <= step - 1 < parts:
            hand_over(step - 1)
        if step == 2:
            lib_copy.wait()
        if step >= 2:
            multiply(step - 2)

    sub = lax.broadcasted_iota(jnp.int32, (8, LANES), 0)

    def as_columns(values):
        upper, lower = values[0], values[8]
        for i in range(1, 8):
            upper = jnp.where(sub == i, values[i], upper)
            lower = jnp.where(sub == i, values[8 + i], lower)
        rest = jnp.zeros((LANES - TOP_K, LANES), F32)
        return jnp.concatenate([upper, lower, rest], axis=0).T

    stride = lib_rows // TOP_K

    def best(tile, carry):
        across = pl.ds(pl.multiple_of(tile * LANES, LANES), LANES)

        def more(r, kept):
            fresh = [
                scores[pl.ds(pl.multiple_of(i * stride + r * 8, 8), 8), across]
                for i in range(TOP_K)
            ]
            return tuple(merge(kept, exchange(fresh, SORT)))

        kept = tuple(jnp.full((8, LANES), -jnp.inf, F32) for _ in range(TOP_K))
        kept = lax.fori_loop(0, stride // 8, more, kept)
        for d in (4, 2, 1):
            kept = merge(kept, [pltpu.roll(x, d, 0) for x in kept])
        outgoing[across, :] = as_columns(kept)
        return carry

    lax.fori_loop(0, total // LANES, best, 0)

    def list_copy(k):
        other = lax.rem(me + k, device_count)
        to_mass, to_shard = other // shard_count, lax.rem(other, shard_count)
        at = ((to_shard // 2) * mass_count + to_mass) * 2 + lax.rem(to_shard, 2)
        return pltpu.make_async_remote_copy(
            src_ref=outgoing.at[pl.ds(pl.multiple_of(at * cap, cap), cap)],
            dst_ref=lists.at[
                pl.ds(pl.multiple_of((shard * mass_count + mass) * cap, cap), cap)
            ],
            send_sem=list_send.at[k],
            recv_sem=list_recv.at[k],
            device_id=(to_mass, to_shard),
            device_id_type=MESH,
        )

    def list_arrival(k):
        other = lax.rem(me + device_count - k, device_count)
        from_mass, from_shard = other // shard_count, lax.rem(other, shard_count)
        return pltpu.make_async_remote_copy(
            src_ref=outgoing.at[pl.ds(0, cap)],
            dst_ref=lists.at[
                pl.ds(pl.multiple_of((from_shard * mass_count + from_mass) * cap, cap), cap)
            ],
            send_sem=list_send.at[k],
            recv_sem=list_recv.at[k],
            device_id=(from_mass, from_shard),
            device_id_type=MESH,
        )

    lax.fori_loop(1, device_count, lambda k, x: (list_copy(k).start(), x)[1], 0)
    own_at = ((place * mass_count + mass) * 2 + core) * cap
    lists[pl.ds(pl.multiple_of((shard * mass_count + mass) * cap, cap), cap), :] = outgoing[
        pl.ds(pl.multiple_of(own_at, cap), cap), :
    ]
    lax.fori_loop(1, device_count, lambda k, x: (list_arrival(k).wait_recv(), x)[1], 0)

    kept = None
    for tile in range(device_count * cap // LANES):
        turned = lists[tile * LANES : (tile + 1) * LANES, :].T
        fresh = [jnp.broadcast_to(turned[i : i + 1, :], (8, LANES)) for i in range(TOP_K)]
        kept = fresh if kept is None else merge(kept, fresh)
    turn = mass_count * cap
    while turn < LANES:
        kept = merge(kept, [pltpu.roll(x, turn, 1) for x in kept])
        turn *= 2
    chosen = jnp.dot(
        owns[...],
        as_columns(kept),
        preferred_element_type=F32,
        precision=lax.Precision.HIGHEST,
    )
    out_ref[...] = chosen

    swap.wait_send()
    swap_hot.wait_send()

    def finish(origin, carry):
        for way, there in (
            (0, (place + 1 < places) & (origin <= place)),
            (1, (place > 0) & (origin >= place)),
        ):

            @pl.when(there)
            def _():
                hot_copy(origin, way).wait_send()
                for part in range(parts):
                    line_copy(origin, part, way).wait_send()

        for part in range(parts):
            for hop in range(1, mass_count):
                layer_copy(origin, part, hop).wait_send()
            pair_copy(origin, part, core).wait_send()
        return carry

    lax.fori_loop(0, places, finish, 0)
    lax.fori_loop(1, device_count, lambda k, x: (list_copy(k).wait_send(), x)[1], 0)


def per_device(mass_count, shard_count, queries, library, routes, offsets):
    rows, bins = queries.shape
    half = bins // 2
    places = shard_count // 2
    cap = rows // 2
    block = mass_count * rows
    total = places * block
    device_count = mass_count * shard_count
    width = half // PARTS
    anywhere = pl.BlockSpec(memory_space=pl.ANY)
    dma = pltpu.SemaphoreType.DMA
    best = pl.pallas_call(
        functools.partial(search_kernel, mass_count, shard_count),
        out_shape=jax.ShapeDtypeStruct((rows, LANES), F32),
        in_specs=[anywhere] * 4,
        out_specs=pl.BlockSpec(memory_space=pltpu.VMEM),
        scratch_shapes=[
            pltpu.VMEM((rows, bins), BF16),
            pltpu.VMEM((1, rows), jnp.int32),
            pltpu.VMEM((1, rows), jnp.int32),
            pltpu.VMEM((2, PARTS, rows, width), BF16),
            pltpu.VMEM((rows, LANES), BF16),
            pltpu.VMEM((rows, LANES), F32),
            pltpu.VMEM(library.shape, BF16),
            pltpu.VMEM((places, PARTS, 2 * rows, width), BF16),
            pltpu.VMEM((places, 2 * rows, LANES), BF16),
            pltpu.VMEM((places, PARTS, block, width), BF16),
            pltpu.VMEM((2, PARTS, total, width), BF16),
            pltpu.VMEM((library.shape[0], total), F32),
            pltpu.VMEM((total, LANES), F32),
            pltpu.VMEM((device_count * cap, LANES), F32),
            dma,
            dma((3,)),
            dma((5,)),
            dma((2, places)),
            dma((places,)),
            dma((2, places * PARTS)),
            dma((places * PARTS,)),
            dma((places * PARTS, mass_count)),
            dma((places * PARTS, mass_count)),
            dma((places * PARTS,)),
            dma((places * PARTS,)),
            dma((device_count,)),
            dma((device_count,)),
        ],
        compiler_params=pltpu.CompilerParams(
            collective_id=0, has_side_effects=True, vmem_limit_bytes=56 * 2**20
        ),
    )(queries, offsets.reshape(1, rows), routes.reshape(1, rows), library)
    return best[:, :TOP_K]


def solution(mesh):
    placed = (
        P(("mass", "shard"), None),
        P(("mass", "shard"), None),
        P(("mass", "shard"), None),
        P(("mass", "shard")),
    )
    return jax.shard_map(
        functools.partial(per_device, mesh.shape["mass"], mesh.shape["shard"]),
        mesh=mesh,
        in_specs=placed,
        out_specs=P(("mass", "shard"), None),
        check_vma=False,
    )
```

time: 60 us -> 53.4 us (0.89)
  local copies, waits for them, and re-layouts: 5.66 us -> 1.3 us
  Pallas kernels: 54.1 us -> 51.9 us
    unnamed x10 -> x1, local copies, waits for them, and re-layouts: 4.93 us -> 1.3 us
    pallas_call x1 -> x0, Pallas kernels: 1.29 us -> none  [per_device(): pl.pallas_call(functools.partial(spectra_kernel, mass_count), out_shape=(...]
    pallas_call x1, Pallas kernels: 52.8 us -> 51.9 us  [per_device(): pl.pallas_call(functools.partial(search_kernel, mass_count, shard_count),...]
    broadcast_in_dim x1 -> x0, local copies, waits for them, and re-layouts: 0.73 us -> none  [per_device(): offsets[:, None]]
where the time goes in v2:
time: 53.4 us; the launch traced here: 53.2 us
  Pallas kernels  51.9 us (97%)
  local copies, waits for them, and re-layouts  1.3 us (2%)
    pallas_call x1, Pallas kernels, per_device(): pl.pallas_call(functools.partial(search_kernel, mass_count, shard_count),...  51.9 us
    unnamed x1, local copies, waits for them, and re-layouts  1.3 us

profile of v2, /device:TPU:0, one launch (start us, length us, event | category | flops | bytes accessed | tf_op | source)
XLA Modules:
  0.0 53.2 jit_solution(15727528981766883175)
XLA Ops:
  0.0 51.9 %shard_map.46 = f32[16,128]{1,0:T(8,128)} custom-call(bf16[16,8192]{1,0:T(8,128)(2,1)} %queries_ref.1, s32[1,16]{1,0:T(1,128)} %bitcast.4, s32[1,16]{1,0:T(1,128)} %bitcast.5, bf16[1024,8192]{1,0:T(8,128)(2,1)} %library_ref.1), custom_call_target="tpu_custom_call" | custom-call | tf_op jit(solution)/shard_map/pallas_call | solution.py:504
  51.9 1.3 %copy.6 = f32[16,16]{1,0:T(8,128)} copy(f32[16,16]{1,0:T(8,128)} %bitcast.3) | data formatting | bytes 2048

commit v3 on v2

--- a/solution.py
+++ b/solution.py
@@ -124,6 +124,8 @@
     scores,
     outgoing,
     lists,
+    merged,
+    homes,
     lib_sem,
     load_sem,
     start_sem,
@@ -137,6 +139,8 @@
     pair_recv,
     list_send,
     list_recv,
+    home_send,
+    home_recv,
 ):
     places = shard_count // 2
     parts, rows, width = halves.shape[1:]
@@ -149,8 +153,6 @@
     place = shard // 2
     core = lax.rem(shard, 2)
     sibling = (mass, shard + 1 - 2 * core)
-    device_count = mass_count * shard_count
-    me = mass * shard_count + shard
 
     loads = [
         pltpu.make_async_copy(source, target, load_sem.at[i])
@@ -163,22 +165,24 @@
     lib_copy = pltpu.make_async_copy(library_ref, lib, lib_sem)
     barrier = pltpu.get_barrier_semaphore()
 
-    def greet(k, carry):
-        other = lax.rem(me + k, device_count)
-        pl.semaphore_signal(
-            barrier,
-            inc=1,
-            device_id=(other // shard_count, lax.rem(other, shard_count)),
-            device_id_type=MESH,
-        )
-        return carry
-
-    lax.fori_loop(1, device_count, greet, 0)
+    def greet(device):
+        pl.semaphore_signal(barrier, inc=1, device_id=device, device_id_type=MESH)
+
+    def mass_peer(k):
+        return (lax.rem(mass + k, mass_count), shard)
+
+    def shard_peer(k):
+        return (mass, lax.rem(shard + k, shard_count))
+
+    for k in range(1, mass_count):
+        greet(mass_peer(k))
+    for k in range(1, shard_count):
+        greet(shard_peer(k))
     for load in loads:
         load.wait()
     lib_copy.start()
     spectra_parts(core, plain, shifts, groups, halves, hots, owns)
-    pl.semaphore_wait(barrier, device_count - 1)
+    pl.semaphore_wait(barrier, mass_count + shard_count - 2)
 
     mine = pl.ds(pl.multiple_of(core * rows, rows), rows)
     swap = pltpu.make_async_remote_copy(
@@ -303,25 +307,16 @@
 
         dispatch(origin, part)
 
-    def gather(part):
-        if part + 2 < parts:
-            leave(part + 2)
-        dispatch(place, part)
-
-        def advance(t, carry):
-            below, above = place - 1 - t, place + 1 + t
-
-            @pl.when(below >= 0)
-            def _():
-                take(below, part, 0, place + 1 < places)
-
-            @pl.when(above < places)
-            def _():
-                take(above, part, 1, place > 0)
-
-            return carry
-
-        lax.fori_loop(0, places - 1, advance, 0)
+    def hop(part, t):
+        below, above = place - 1 - t, place + 1 + t
+
+        @pl.when(below >= 0)
+        def _():
+            take(below, part, 0, place + 1 < places)
+
+        @pl.when(above < places)
+        def _():
+            take(above, part, 1, place > 0)
 
     def hand_over(part):
         def one(origin):
@@ -371,15 +366,38 @@
 
     for part in range(min(2, parts)):
         leave(part)
-    for step in range(parts + 2):
-        if step < parts:
-            gather(step)
-        if 0 <= step - 1 < parts:
-            hand_over(step - 1)
-        if step == 2:
+
+    def fill(step, carry):
+        for part in range(2, parts):
+
+            @pl.when(step == part - 2)
+            def _():
+                leave(part)
+
+        for part in range(parts):
+
+            @pl.when((step > part) & (step - part < places))
+            def _():
+                hop(part, step - 1 - part)
+
+            @pl.when(step == part)
+            def _():
+                dispatch(place, part)
+
+        return carry
+
+    steady = max(places, parts)
+    lax.fori_loop(0, steady, fill, 0)
+    for step in range(steady, steady + parts + 1):
+        for part in range(parts):
+            if 0 <= step - 1 - part < places - 1:
+                hop(part, step - 1 - part)
+        if step - steady < parts:
+            hand_over(step - steady)
+        if step == steady + 1:
             lib_copy.wait()
-        if step >= 2:
-            multiply(step - 2)
+        if step > steady:
+            multiply(step - steady - 1)
 
     sub = lax.broadcasted_iota(jnp.int32, (8, LANES), 0)
 
@@ -407,59 +425,94 @@
         kept = lax.fori_loop(0, stride // 8, more, kept)
         for d in (4, 2, 1):
             kept = merge(kept, [pltpu.roll(x, d, 0) for x in kept])
-        outgoing[across, :] = as_columns(kept)
+        columns = as_columns(kept)
+        for i in range(LANES // block):
+            for m in range(mass_count):
+                for c in range(2):
+                    at = i * block + m * rows + c * cap
+                    outgoing[tile * (LANES // block) + i, c, m * cap : (m + 1) * cap, :] = columns[
+                        at : at + cap
+                    ]
         return carry
 
     lax.fori_loop(0, total // LANES, best, 0)
 
+    list_rows = mass_count * cap
+
     def list_copy(k):
-        other = lax.rem(me + k, device_count)
-        to_mass, to_shard = other // shard_count, lax.rem(other, shard_count)
-        at = ((to_shard // 2) * mass_count + to_mass) * 2 + lax.rem(to_shard, 2)
-        return pltpu.make_async_remote_copy(
-            src_ref=outgoing.at[pl.ds(pl.multiple_of(at * cap, cap), cap)],
-            dst_ref=lists.at[
-                pl.ds(pl.multiple_of((shard * mass_count + mass) * cap, cap), cap)
-            ],
+        target = shard_peer(k)
+        return pltpu.make_async_remote_copy(
+            src_ref=outgoing.at[target[1] // 2, lax.rem(target[1], 2)],
+            dst_ref=lists.at[pl.ds(pl.multiple_of(shard * list_rows, list_rows), list_rows)],
             send_sem=list_send.at[k],
             recv_sem=list_recv.at[k],
-            device_id=(to_mass, to_shard),
+            device_id=target,
             device_id_type=MESH,
         )
 
     def list_arrival(k):
-        other = lax.rem(me + device_count - k, device_count)
-        from_mass, from_shard = other // shard_count, lax.rem(other, shard_count)
-        return pltpu.make_async_remote_copy(
-            src_ref=outgoing.at[pl.ds(0, cap)],
-            dst_ref=lists.at[
-                pl.ds(pl.multiple_of((from_shard * mass_count + from_mass) * cap, cap), cap)
-            ],
+        source = shard_peer(shard_count - k)
+        return pltpu.make_async_remote_copy(
+            src_ref=outgoing.at[0, 0],
+            dst_ref=lists.at[pl.ds(pl.multiple_of(source[1] * list_rows, list_rows), list_rows)],
             send_sem=list_send.at[k],
             recv_sem=list_recv.at[k],
-            device_id=(from_mass, from_shard),
-            device_id_type=MESH,
-        )
-
-    lax.fori_loop(1, device_count, lambda k, x: (list_copy(k).start(), x)[1], 0)
-    own_at = ((place * mass_count + mass) * 2 + core) * cap
-    lists[pl.ds(pl.multiple_of((shard * mass_count + mass) * cap, cap), cap), :] = outgoing[
-        pl.ds(pl.multiple_of(own_at, cap), cap), :
+            device_id=source,
+            device_id_type=MESH,
+        )
+
+    for k in range(1, shard_count):
+        list_copy(k).start()
+    lists[pl.ds(pl.multiple_of(shard * list_rows, list_rows), list_rows), :] = outgoing[
+        place, core
     ]
-    lax.fori_loop(1, device_count, lambda k, x: (list_arrival(k).wait_recv(), x)[1], 0)
+    for k in range(1, shard_count):
+        list_arrival(k).wait_recv()
 
     kept = None
-    for tile in range(device_count * cap // LANES):
+    for tile in range(shard_count * list_rows // LANES):
         turned = lists[tile * LANES : (tile + 1) * LANES, :].T
         fresh = [jnp.broadcast_to(turned[i : i + 1, :], (8, LANES)) for i in range(TOP_K)]
         kept = fresh if kept is None else merge(kept, fresh)
-    turn = mass_count * cap
+    turn = list_rows
     while turn < LANES:
         kept = merge(kept, [pltpu.roll(x, turn, 1) for x in kept])
         turn *= 2
+    merged[...] = as_columns(kept)[:list_rows]
+
+    def group_rows(m):
+        return pl.ds(pl.multiple_of(m * cap, cap), cap)
+
+    def home_copy(k):
+        target = mass_peer(k)
+        return pltpu.make_async_remote_copy(
+            src_ref=merged.at[group_rows(target[0])],
+            dst_ref=homes.at[group_rows(mass)],
+            send_sem=home_send.at[k],
+            recv_sem=home_recv.at[k],
+            device_id=target,
+            device_id_type=MESH,
+        )
+
+    def home_arrival(k):
+        source = mass_peer(mass_count - k)
+        return pltpu.make_async_remote_copy(
+            src_ref=merged.at[pl.ds(0, cap)],
+            dst_ref=homes.at[group_rows(source[0])],
+            send_sem=home_send.at[k],
+            recv_sem=home_recv.at[k],
+            device_id=source,
+            device_id_type=MESH,
+        )
+
+    for k in range(1, mass_count):
+        home_copy(k).start()
+    homes[group_rows(mass), :] = merged[group_rows(mass), :]
+    for k in range(1, mass_count):
+        home_arrival(k).wait_recv()
     chosen = jnp.dot(
-        owns[...],
-        as_columns(kept),
+        owns[:, :list_rows],
+        homes[...],
         preferred_element_type=F32,
         precision=lax.Precision.HIGHEST,
     )
@@ -487,7 +540,10 @@
         return carry
 
     lax.fori_loop(0, places, finish, 0)
-    lax.fori_loop(1, device_count, lambda k, x: (list_copy(k).wait_send(), x)[1], 0)
+    for k in range(1, shard_count):
+        list_copy(k).wait_send()
+    for k in range(1, mass_count):
+        home_copy(k).wait_send()
 
 
 def per_device(mass_count, shard_count, queries, library, routes, offsets):
@@ -497,7 +553,6 @@
     cap = rows // 2
     block = mass_count * rows
     total = places * block
-    device_count = mass_count * shard_count
     width = half // PARTS
     anywhere = pl.BlockSpec(memory_space=pl.ANY)
     dma = pltpu.SemaphoreType.DMA
@@ -519,8 +574,10 @@
             pltpu.VMEM((places, PARTS, block, width), BF16),
             pltpu.VMEM((2, PARTS, total, width), BF16),
             pltpu.VMEM((library.shape[0], total), F32),
-            pltpu.VMEM((total, LANES), F32),
-            pltpu.VMEM((device_count * cap, LANES), F32),
+            pltpu.VMEM((places, 2, mass_count * cap, LANES), F32),
+            pltpu.VMEM((shard_count * mass_count * cap, LANES), F32),
+            pltpu.VMEM((mass_count * cap, LANES), F32),
+            pltpu.VMEM((mass_count * cap, LANES), F32),
             dma,
             dma((3,)),
             dma((5,)),
@@ -532,8 +589,10 @@
             dma((places * PARTS, mass_count)),
             dma((places * PARTS,)),
             dma((places * PARTS,)),
-            dma((device_count,)),
-            dma((device_count,)),
+            dma((shard_count,)),
+            dma((shard_count,)),
+            dma((mass_count,)),
+            dma((mass_count,)),
         ],
         compiler_params=pltpu.CompilerParams(
             collective_id=0, has_side_effects=True, vmem_limit_bytes=56 * 2**20

time: 53.4 us -> 52.3 us (0.979)
  Pallas kernels: 51.9 us -> 50.8 us
    pallas_call x1, Pallas kernels: 51.9 us -> 50.8 us  [per_device(): pl.pallas_call(functools.partial(search_kernel, mass_count, shard_count),...]
where the time goes in v3:
time: 52.3 us; the launch traced here: 52.1 us
  Pallas kernels  50.8 us (97%)
  local copies, waits for them, and re-layouts  1.3 us (2%)
    pallas_call x1, Pallas kernels, per_device(): pl.pallas_call(functools.partial(search_kernel, mass_count, shard_count),...  50.8 us
    unnamed x1, local copies, waits for them, and re-layouts  1.3 us

profile of v3, /device:TPU:0, one launch (start us, length us, event | category | flops | bytes accessed | tf_op | source)
XLA Modules:
  0.0 52.1 jit_solution(13127981212478269586)
XLA Ops:
  0.0 50.8 %shard_map.46 = f32[16,128]{1,0:T(8,128)} custom-call(bf16[16,8192]{1,0:T(8,128)(2,1)} %queries_ref.1, s32[1,16]{1,0:T(1,128)} %bitcast.4, s32[1,16]{1,0:T(1,128)} %bitcast.5, bf16[1024,8192]{1,0:T(8,128)(2,1)} %library_ref.1), custom_call_target="tpu_custom_call" | custom-call | tf_op jit(solution)/shard_map/pallas_call | solution.py:559
  50.8 1.3 %copy.6 = f32[16,16]{1,0:T(8,128)} copy(f32[16,16]{1,0:T(8,128)} %bitcast.3) | data formatting | bytes 2048

commit v4 on v3

--- a/solution.py
+++ b/solution.py
@@ -318,6 +318,48 @@
         def _():
             take(above, part, 1, place > 0)
 
+    def slots_copy(origin, part, way):
+        span = slots.at[core, part, pl.ds(pl.multiple_of(origin * block, block), block)]
+        return pltpu.make_async_remote_copy(
+            src_ref=span,
+            dst_ref=span,
+            send_sem=line_send.at[way, origin * parts + part],
+            recv_sem=line_recv.at[origin * parts + part],
+            device_id=(mass, shard + (2 if way == 0 else -2)),
+            device_id_type=MESH,
+        )
+
+    def leave_slots(part):
+        for hop in range(1, mass_count):
+            layer_arrival(place, part, hop).wait_recv()
+        for way, there in ((0, place + 1 < places), (1, place > 0)):
+
+            @pl.when(there)
+            def _():
+                slots_copy(place, part, way).start()
+
+        pair_copy(place, part, core).start()
+
+    def take_slots(origin, part, way, there):
+        slots_copy(origin, part, way).wait_recv()
+
+        @pl.when(there)
+        def _():
+            slots_copy(origin, part, way).start()
+
+        pair_copy(origin, part, core).start()
+
+    def hop_slots(part, t):
+        below, above = place - 1 - t, place + 1 + t
+
+        @pl.when(below >= 0)
+        def _():
+            take_slots(below, part, 0, place + 1 < places)
+
+        @pl.when(above < places)
+        def _():
+            take_slots(above, part, 1, place > 0)
+
     def hand_over(part):
         def one(origin):
             for hop in range(1, mass_count):
@@ -364,17 +406,20 @@
 
         lax.fori_loop(0, (lib_rows // tall) * (total // wide), score, 0)
 
-    for part in range(min(2, parts)):
+    for part in range(2):
         leave(part)
 
+    turned = parts - 1
+    dispatch(place, turned)
+
     def fill(step, carry):
-        for part in range(2, parts):
+        for part in range(2, turned):
 
             @pl.when(step == part - 2)
             def _():
                 leave(part)
 
-        for part in range(parts):
+        for part in range(turned):
 
             @pl.when((step > part) & (step - part < places))
             def _():
@@ -384,18 +429,30 @@
             def _():
                 dispatch(place, part)
 
+        @pl.when(step == 1)
+        def _():
+            leave_slots(turned)
+
+        @pl.when((step > 1) & (step - 2 < places - 1))
+        def _():
+            hop_slots(turned, step - 2)
+
         return carry
 
     steady = max(places, parts)
     lax.fori_loop(0, steady, fill, 0)
-    for step in range(steady, steady + parts + 1):
-        for part in range(parts):
+    for step in range(steady, steady + turned + 1):
+        for part in range(turned):
             if 0 <= step - 1 - part < places - 1:
                 hop(part, step - 1 - part)
-        if step - steady < parts:
+        if step - 2 < places - 1:
+            hop_slots(turned, step - 2)
+        if step - steady < turned:
             hand_over(step - steady)
         if step == steady + 1:
             lib_copy.wait()
+        if step == steady + turned:
+            multiply(turned)
         if step > steady:
             multiply(step - steady - 1)
 
@@ -471,8 +528,8 @@
 
     kept = None
     for tile in range(shard_count * list_rows // LANES):
-        turned = lists[tile * LANES : (tile + 1) * LANES, :].T
-        fresh = [jnp.broadcast_to(turned[i : i + 1, :], (8, LANES)) for i in range(TOP_K)]
+        upright = lists[tile * LANES : (tile + 1) * LANES, :].T
+        fresh = [jnp.broadcast_to(upright[i : i + 1, :], (8, LANES)) for i in range(TOP_K)]
         kept = fresh if kept is None else merge(kept, fresh)
     turn = list_rows
     while turn < LANES:
@@ -530,12 +587,20 @@
             @pl.when(there)
             def _():
                 hot_copy(origin, way).wait_send()
-                for part in range(parts):
+                for part in range(turned):
                     line_copy(origin, part, way).wait_send()
-
-        for part in range(parts):
+                slots_copy(origin, turned, way).wait_send()
+
+        for part in range(turned):
             for hop in range(1, mass_count):
                 layer_copy(origin, part, hop).wait_send()
+
+        @pl.when(origin == place)
+        def _():
+            for hop in range(1, mass_count):
+                layer_copy(origin, turned, hop).wait_send()
+
+        for part in range(parts):
             pair_copy(origin, part, core).wait_send()
         return carry
 

time: 52.3 us -> 50.9 us (0.973)
  Pallas kernels: 50.8 us -> 49.4 us
    pallas_call x1, Pallas kernels: 50.8 us -> 49.4 us  [per_device(): pl.pallas_call(functools.partial(search_kernel, mass_count, shard_count),...]
where the time goes in v4:
time: 50.9 us; the launch traced here: 50.7 us
  Pallas kernels  49.4 us (97%)
  local copies, waits for them, and re-layouts  1.3 us (3%)
    pallas_call x1, Pallas kernels, per_device(): pl.pallas_call(functools.partial(search_kernel, mass_count, shard_count),...  49.4 us
    unnamed x1, local copies, waits for them, and re-layouts  1.3 us

profile of v4, /device:TPU:0, one launch (start us, length us, event | category | flops | bytes accessed | tf_op | source)
XLA Modules:
  0.0 50.7 jit_solution(3478861095138634005)
XLA Ops:
  0.0 49.4 %shard_map.46 = f32[16,128]{1,0:T(8,128)} custom-call(bf16[16,8192]{1,0:T(8,128)(2,1)} %queries_ref.1, s32[1,16]{1,0:T(1,128)} %bitcast.4, s32[1,16]{1,0:T(1,128)} %bitcast.5, bf16[1024,8192]{1,0:T(8,128)(2,1)} %library_ref.1), custom_call_target="tpu_custom_call" | custom-call | tf_op jit(solution)/shard_map/pallas_call | solution.py:624
  49.4 1.3 %copy.6 = f32[16,16]{1,0:T(8,128)} copy(f32[16,16]{1,0:T(8,128)} %bitcast.3) | data formatting | bytes 2048

commit v5 on v4

--- a/solution.py
+++ b/solution.py
@@ -266,7 +266,7 @@
             device_id_type=MESH,
         )
 
-    tile = min(512, width)
+    tile = width
 
     def dispatch(origin, part):
         hot = held_hots[origin].astype(F32).T[:block].astype(BF16)
@@ -380,7 +380,7 @@
         lax.fori_loop(0, places - 1, advance, 0)
 
     lib_rows = lib.shape[0]
-    tall, wide = min(512, lib_rows), min(256, total)
+    tall, wide = lib_rows, min(256, total)
 
     def multiply(part):
         lax.fori_loop(

time: 50.9 us -> 52.8 us (1.037)
  Pallas kernels: 49.4 us -> 51.3 us
    pallas_call x1, Pallas kernels: 49.4 us -> 51.3 us  [per_device(): pl.pallas_call(functools.partial(search_kernel, mass_count, shard_count),...]
where the time goes in v5:
time: 52.8 us; the launch traced here: 52.6 us
  Pallas kernels  51.3 us (97%)
  local copies, waits for them, and re-layouts  1.3 us (2%)
    pallas_call x1, Pallas kernels, per_device(): pl.pallas_call(functools.partial(search_kernel, mass_count, shard_count),...  51.3 us
    unnamed x1, local copies, waits for them, and re-layouts  1.3 us

profile of v5, /device:TPU:0, one launch (start us, length us, event | category | flops | bytes accessed | tf_op | source)
XLA Modules:
  0.0 52.6 jit_solution(1058995132129248937)
XLA Ops:
  0.0 51.3 %shard_map.46 = f32[16,128]{1,0:T(8,128)} custom-call(bf16[16,8192]{1,0:T(8,128)(2,1)} %queries_ref.1, s32[1,16]{1,0:T(1,128)} %bitcast.4, s32[1,16]{1,0:T(1,128)} %bitcast.5, bf16[1024,8192]{1,0:T(8,128)(2,1)} %library_ref.1), custom_call_target="tpu_custom_call" | custom-call | tf_op jit(solution)/shard_map/pallas_call | solution.py:624
  51.3 1.3 %copy.6 = f32[16,16]{1,0:T(8,128)} copy(f32[16,16]{1,0:T(8,128)} %bitcast.3) | data formatting | bytes 2048
